TPU v7x, 32 devices: a whole 2x2x4 slice. The times are simulated.
32 devices in a mesh: branch: 2 (over y), dp: 16 (over z, x, core).
Axes of the slice: x: 2, y: 2, z: 4, core: 2. Of those that a mesh axis runs over, the one named last changes fastest.
Arguments:
- hidden: bfloat16 [64, 512, 768], P('dp'), may hold values from -6 to 6
- bounds: int32 [64, 2], P('dp'), may hold values from 1 to 512, as said below
- query_weight: bfloat16 [768, 384], replicated, may hold values from -0.21875 to 0.21875
- query_bias: float32 [384], replicated, may hold values from -3 to 3
- branch_keys: bfloat16 [2, 768, 384], P('branch'), may hold values from -0.21875 to 0.21875
- branch_values: bfloat16 [2, 768, 384], P('branch'), may hold values from -0.875 to 0.875
- branch_bias: float32 [2, 384], P('branch'), may hold values from -6 to 6
- depth_kernel: float32 [9, 768], replicated, may hold values from -2 to 2
- point_bias: float32 [384], replicated, may hold values from -3 to 3
- kernel_weight: bfloat16 [384, 54], replicated, may hold values from -0.3125 to 0.3125
- kernel_bias: float32 [54], replicated, may hold values from -3 to 3
- mixer_weight: bfloat16 [768, 768], replicated, may hold values from -0.21875 to 0.21875
- mixer_bias: float32 [768], replicated, may hold values from -3 to 3
- first_gain: float32 [768], replicated, may hold values from 0.1 to 1.9
- first_shift: float32 [768], replicated, may hold values from -3 to 3
- inner_weight: bfloat16 [2, 384, 1536], replicated, may hold values from -0.3125 to 0.3125
- inner_bias: float32 [3072], replicated, may hold values from -3 to 3
- outer_weight: bfloat16 [2, 1536, 384], replicated, may hold values from -0.15625 to 0.15625
- outer_bias: float32 [768], replicated, may hold values from -3 to 3
- second_gain: float32 [768], replicated, may hold values from 0.1 to 1.9
- second_shift: float32 [768], replicated, may hold values from -3 to 3
- cotangent: bfloat16 [64, 512, 768], P('dp', 'branch'), may hold values from -6 to 6
Outputs:
- output: bfloat16 [64, 512, 768], P('dp', 'branch')
- hidden_grad: float32 [64, 512, 768], P('dp', 'branch')
- query_weight_grad: float32 [768, 384], replicated
- query_bias_grad: float32 [384], replicated
- branch_keys_grad: float32 [2, 768, 384], P('branch')
- branch_values_grad: float32 [2, 768, 384], P('branch')
- branch_bias_grad: float32 [2, 384], P('branch')
- depth_kernel_grad: float32 [9, 768], replicated
- point_bias_grad: float32 [384], replicated
- kernel_weight_grad: float32 [384, 54], replicated
- kernel_bias_grad: float32 [54], replicated
- mixer_weight_grad: float32 [768, 768], replicated
- mixer_bias_grad: float32 [768], replicated
- first_gain_grad: float32 [768], replicated
- first_shift_grad: float32 [768], replicated
- inner_weight_grad: float32 [2, 384, 1536], replicated
- inner_bias_grad: float32 [3072], replicated
- outer_weight_grad: float32 [2, 1536, 384], replicated
- outer_bias_grad: float32 [768], replicated
- second_gain_grad: float32 [768], replicated
- second_shift_grad: float32 [768], replicated
Inputs may be any that keep to these rules, and one draw needn't show every extreme that they name: `bounds`: column 0 of a row is the position of its first segment's separator and column 1 its count of valid positions: 1 <= column 0 <= column 1 - 2 and 128 <= column 1; some row has 512 valid positions.
All inputs are finite; a program needn't handle non-finite values.
Results may differ from a plain program's by a relative error of at most 0.02.
Values may be sent and summed in bfloat16 or wider, within the bound.
No kernel may reach another device: no remote copies, remote signals or barrier semaphores. Data moves between devices by JAX's collectives and lax.ppermute only.
A program may use at most 256 MiB of HBM per device.

v0:
```python
import jax
import jax.numpy as jnp
from jax import lax
from jax.sharding import PartitionSpec as P

HEADS = 6
HEAD_SIZE = 64
GROUPS = 2
KERNEL = 9


NEGATIVE = -1000000000.0
EPSILON = 1e-05
ROOT_HALF = 0.7071067811865476
INV_ROOT_TAU = 0.3989422804014327


def shifted(source, offset, filler, radius):
    padding = [(0, 0)] * source.ndim
    padding[1] = (radius, radius)
    padded = jnp.pad(source, padding, constant_values=filler)
    return lax.slice_in_dim(padded, radius + offset, radius + offset + source.shape[1], axis=1)


def project(source, matrix):
    return jnp.einsum("rsd,de->rse", source, matrix, preferred_element_type=jnp.float32)


def weight_grad(source, gradient):
    return jnp.einsum("rsd,rse->de", source, gradient, preferred_element_type=jnp.float32)


def back_project(gradient, matrix):
    return jnp.einsum("rse,de->rsd", gradient, matrix, preferred_element_type=jnp.float32)


def column_sum(gradient):
    return jnp.sum(gradient.astype(jnp.float32), axis=(0, 1))


def grouped(source, matrix):
    row_count, length = (source.shape[0], source.shape[1])
    split_source = source.reshape(row_count, length, matrix.shape[0], matrix.shape[1])
    return jnp.einsum(
        "rsgi,gio->rsgo", split_source, matrix, preferred_element_type=jnp.float32
    ).reshape(row_count, length, -1)


def group_grad(source, gradient, groups):
    row_count, length = (source.shape[0], source.shape[1])
    split_source = source.reshape(row_count, length, groups, -1)
    split_grad = gradient.reshape(row_count, length, groups, -1)
    return jnp.einsum(
        "rsgi,rsgo->gio", split_source, split_grad, preferred_element_type=jnp.float32
    )


def group_back(gradient, matrix):
    row_count, length = (gradient.shape[0], gradient.shape[1])
    split_grad = gradient.reshape(row_count, length, matrix.shape[0], matrix.shape[2])
    return jnp.einsum(
        "rsgo,gio->rsgi", split_grad, matrix, preferred_element_type=jnp.float32
    ).reshape(row_count, length, -1)


def softmax_last(scores):
    row_peak = jnp.max(scores, axis=-1, keepdims=True)
    raised = jnp.exp(scores - row_peak)
    return raised / jnp.sum(raised, axis=-1, keepdims=True)


def normalize(source):
    center = source - jnp.mean(source, axis=-1, keepdims=True)
    spread = jnp.mean(center * center, axis=-1, keepdims=True)
    factor = lax.rsqrt(spread + EPSILON)
    return (center * factor, factor)


def norm_back(gradient, normed, factor):
    return factor * (
        gradient
        - jnp.mean(gradient, axis=-1, keepdims=True)
        - normed * jnp.mean(gradient * normed, axis=-1, keepdims=True)
    )


def segment_ids(bounds, length):
    position = jnp.arange(length, dtype=jnp.int32)[None, :]
    inner_ids = jnp.where(position < bounds[:, 1:2], 1, 2)
    return jnp.where(position <= bounds[:, 0:1], 0, inner_ids).astype(jnp.int32)


def attention_parts(
    hidden, query_source, bounds, query_weight, query_bias, key_weight, value_weight, value_bias
):
    row_count, length = (hidden.shape[0], hidden.shape[1])
    query_length = query_source.shape[1]
    queries = (project(query_source, query_weight) + query_bias).astype(jnp.bfloat16)
    queries = queries.reshape(row_count, query_length, HEADS, HEAD_SIZE)
    key_rows = (
        project(hidden, key_weight)
        .astype(jnp.bfloat16)
        .reshape(row_count, length, HEADS, HEAD_SIZE)
    )
    valued = (project(hidden, value_weight) + value_bias).astype(jnp.bfloat16)
    valued = valued.reshape(row_count, length, HEADS, HEAD_SIZE)
    scores = jnp.einsum(
        "rqhe,rkhe->rhqk", queries, key_rows, preferred_element_type=jnp.float32
    ) * HEAD_SIZE ** (-0.5)
    position = jnp.arange(length, dtype=jnp.int32)
    visible = position[None, None, None, :] < bounds[:, 1][:, None, None, None]
    attend_weights = softmax_last(jnp.where(visible, scores, NEGATIVE))
    return (queries, key_rows, valued, attend_weights)


def attention_forward(
    hidden, query_source, bounds, query_weight, query_bias, key_weight, value_weight, value_bias
):
    row_count, query_length = (query_source.shape[0], query_source.shape[1])
    queries, key_rows, valued, attend_weights = attention_parts(
        hidden, query_source, bounds, query_weight, query_bias, key_weight, value_weight, value_bias
    )
    attended = jnp.einsum(
        "rhqk,rkhe->rqhe",
        attend_weights.astype(jnp.bfloat16),
        valued,
        preferred_element_type=jnp.float32,
    )
    return attended.reshape(row_count, query_length, -1).astype(jnp.bfloat16)


def attention_core(
    hidden,
    query_source,
    bounds,
    gradient,
    query_weight,
    query_bias,
    key_weight,
    value_weight,
    value_bias,
):
    row_count, length = (hidden.shape[0], hidden.shape[1])
    query_length = query_source.shape[1]
    scaling = HEAD_SIZE ** (-0.5)
    queries, key_rows, valued, attend_weights = attention_parts(
        hidden, query_source, bounds, query_weight, query_bias, key_weight, value_weight, value_bias
    )
    grad_heads = gradient.reshape(row_count, query_length, HEADS, HEAD_SIZE)
    grad_value = jnp.einsum(
        "rhqk,rqhe->rkhe",
        attend_weights.astype(jnp.bfloat16),
        grad_heads,
        preferred_element_type=jnp.float32,
    ).reshape(row_count, length, -1)
    grad_probs = jnp.einsum(
        "rqhe,rkhe->rhqk", grad_heads, valued, preferred_element_type=jnp.float32
    )
    grad_scores = attend_weights * (
        grad_probs - jnp.sum(grad_probs * attend_weights, axis=-1, keepdims=True)
    )
    grad_scores = grad_scores.astype(jnp.bfloat16)
    grad_query = (
        jnp.einsum("rhqk,rkhe->rqhe", grad_scores, key_rows, preferred_element_type=jnp.float32)
        * scaling
    )
    grad_query = grad_query.astype(jnp.bfloat16).reshape(row_count, query_length, -1)
    grad_key = (
        jnp.einsum("rhqk,rqhe->rkhe", grad_scores, queries, preferred_element_type=jnp.float32)
        * scaling
    )
    grad_key = grad_key.reshape(row_count, length, -1)
    return (grad_query, grad_key, grad_value)


def attention_backward(
    hidden,
    bounds,
    gradient,
    query_weight,
    query_bias,
    key_weight,
    value_weight,
    value_bias,
    depth_kernel,
    point_bias,
    kernel_weight,
    kernel_bias,
):
    grad_query, grad_key, grad_value = attention_core(
        hidden,
        hidden,
        bounds,
        gradient,
        query_weight,
        query_bias,
        key_weight,
        value_weight,
        value_bias,
    )
    grad_key = grad_key.astype(jnp.bfloat16)
    grad_value = grad_value.astype(jnp.bfloat16)
    hidden_part = (
        back_project(grad_query, query_weight)
        + back_project(grad_key, key_weight)
        + back_project(grad_value, value_weight)
    )
    return (
        hidden_part,
        weight_grad(hidden, grad_query),
        column_sum(grad_query),
        weight_grad(hidden, grad_key),
        weight_grad(hidden, grad_value),
        column_sum(grad_value),
        jnp.zeros_like(depth_kernel),
        jnp.zeros_like(point_bias),
        jnp.zeros(kernel_weight.shape, jnp.float32),
        jnp.zeros_like(kernel_bias),
    )


def convolution_parts(
    hidden,
    bounds,
    query_weight,
    query_bias,
    depth_kernel,
    point_weight,
    point_bias,
    kernel_weight,
    kernel_bias,
    value_weight,
    value_bias,
):
    row_count, length = (hidden.shape[0], hidden.shape[1])
    radius = KERNEL // 2
    queries = (project(hidden, query_weight) + query_bias).astype(jnp.bfloat16)
    depth_sum = jnp.zeros(hidden.shape, jnp.float32)
    for tap_index in range(KERNEL):
        depth_sum = (
            depth_sum
            + shifted(hidden, tap_index - radius, 0, radius).astype(jnp.float32)
            * depth_kernel[tap_index]
        )
    depth_mixed = depth_sum.astype(jnp.bfloat16)
    key_kernel = project(depth_mixed, point_weight) + point_bias
    joint_key = (key_kernel * queries.astype(jnp.float32)).astype(jnp.bfloat16)
    logits = (
        jnp.einsum("rsa,ac->rsc", joint_key, kernel_weight, preferred_element_type=jnp.float32)
        + kernel_bias
    )
    logits = logits.reshape(row_count, length, HEADS, KERNEL)
    segment = segment_ids(bounds, length)
    same_segment = jnp.stack(
        [
            shifted(segment, tap_index - radius, -1, radius) == segment
            for tap_index in range(KERNEL)
        ],
        axis=-1,
    )
    tap_weights = softmax_last(jnp.where(same_segment[:, :, None, :], logits, NEGATIVE))
    valued = (project(hidden, value_weight) + value_bias).astype(jnp.bfloat16)
    valued = valued.reshape(row_count, length, HEADS, HEAD_SIZE)
    return (queries, depth_mixed, key_kernel, joint_key, tap_weights, valued)


def convolution_forward(
    hidden,
    bounds,
    query_weight,
    query_bias,
    depth_kernel,
    point_weight,
    point_bias,
    kernel_weight,
    kernel_bias,
    value_weight,
    value_bias,
):
    row_count, length = (hidden.shape[0], hidden.shape[1])
    radius = KERNEL // 2
    queries, depth_mixed, key_kernel, joint_key, tap_weights, valued = convolution_parts(
        hidden,
        bounds,
        query_weight,
        query_bias,
        depth_kernel,
        point_weight,
        point_bias,
        kernel_weight,
        kernel_bias,
        value_weight,
        value_bias,
    )
    conv_sum = jnp.zeros(valued.shape, jnp.float32)
    for tap_index in range(KERNEL):
        conv_sum = conv_sum + tap_weights[..., tap_index : tap_index + 1] * shifted(
            valued, tap_index - radius, 0, radius
        ).astype(jnp.float32)
    return conv_sum.reshape(row_count, length, -1).astype(jnp.bfloat16)


def convolution_backward(
    hidden,
    bounds,
    gradient,
    keep,
    query_weight,
    query_bias,
    depth_kernel,
    point_weight,
    point_bias,
    kernel_weight,
    kernel_bias,
    value_weight,
    value_bias,
):
    row_count, length = (hidden.shape[0], hidden.shape[1])
    radius = KERNEL // 2
    queries, depth_mixed, key_kernel, joint_key, tap_weights, valued = convolution_parts(
        hidden,
        bounds,
        query_weight,
        query_bias,
        depth_kernel,
        point_weight,
        point_bias,
        kernel_weight,
        kernel_bias,
        value_weight,
        value_bias,
    )
    grad_heads = gradient.astype(jnp.float32).reshape(row_count, length, HEADS, HEAD_SIZE)
    grad_taps = jnp.stack(
        [
            jnp.sum(
                grad_heads * shifted(valued, tap_index - radius, 0, radius).astype(jnp.float32),
                axis=-1,
            )
            for tap_index in range(KERNEL)
        ],
        axis=-1,
    )
    grad_valued = jnp.zeros(grad_heads.shape, jnp.float32)
    for tap_index in range(KERNEL):
        grad_valued = grad_valued + shifted(
            tap_weights[..., tap_index : tap_index + 1] * grad_heads,
            radius - tap_index,
            0.0,
            radius,
        )
    grad_valued = grad_valued.astype(jnp.bfloat16).reshape(row_count, length, -1)
    grad_logits = tap_weights * (
        grad_taps - jnp.sum(grad_taps * tap_weights, axis=-1, keepdims=True)
    )
    grad_logits = grad_logits.astype(jnp.bfloat16).reshape(row_count, length, -1)
    grad_joint = back_project(grad_logits, kernel_weight).astype(jnp.bfloat16).astype(jnp.float32)
    grad_key = (grad_joint * queries.astype(jnp.float32)).astype(jnp.bfloat16)
    grad_query = (grad_joint * key_kernel).astype(jnp.bfloat16)
    grad_depth_mixed = back_project(grad_key, point_weight).astype(jnp.bfloat16).astype(jnp.float32)
    hidden_part = back_project(grad_query, query_weight) + back_project(grad_valued, value_weight)
    for tap_index in range(KERNEL):
        hidden_part = hidden_part + shifted(
            grad_depth_mixed * depth_kernel[tap_index], radius - tap_index, 0.0, radius
        )
    kept_logits = grad_logits * keep
    kept_key = grad_key * keep
    kept_query = grad_query * keep
    kept_valued = grad_valued * keep
    kept_depth = grad_depth_mixed * keep.astype(jnp.float32)
    grad_kernel = weight_grad(joint_key, kept_logits)
    grad_kernel_bias = column_sum(kept_logits)
    grad_point = weight_grad(depth_mixed, kept_key)
    grad_point_bias = column_sum(kept_key)
    grad_depth = jnp.stack(
        [
            jnp.sum(
                shifted(hidden, tap_index - radius, 0, radius).astype(jnp.float32) * kept_depth,
                axis=(0, 1),
            )
            for tap_index in range(KERNEL)
        ],
        axis=0,
    )
    return (
        hidden_part,
        weight_grad(hidden, kept_query),
        column_sum(kept_query),
        grad_point,
        weight_grad(hidden, kept_valued),
        column_sum(kept_valued),
        grad_depth,
        grad_point_bias,
        grad_kernel,
        grad_kernel_bias,
    )


def shards(
    hidden,
    bounds,
    query_weight,
    query_bias,
    branch_keys,
    branch_values,
    branch_bias,
    depth_kernel,
    point_bias,
    kernel_weight,
    kernel_bias,
    mixer_weight,
    mixer_bias,
    first_gain,
    first_shift,
    inner_weight,
    inner_bias,
    outer_weight,
    outer_bias,
    second_gain,
    second_shift,
    cotangent,
):
    branch_side = lax.axis_index("branch")
    half_length = cotangent.shape[1]
    full_length = hidden.shape[1]
    own_start = branch_side * half_length
    own_hidden = lax.dynamic_slice_in_dim(hidden, own_start, half_length, 1)
    key_weight = branch_keys[0]
    value_weight = branch_values[0]
    value_bias = branch_bias[0]

    def attention_out():
        return attention_forward(
            hidden, hidden, bounds, query_weight, query_bias, key_weight, value_weight, value_bias
        )

    def kernel_out():
        return convolution_forward(
            hidden,
            bounds,
            query_weight,
            query_bias,
            depth_kernel,
            key_weight,
            point_bias,
            kernel_weight,
            kernel_bias,
            value_weight,
            value_bias,
        )

    branch_out = lax.cond(branch_side == 0, attention_out, kernel_out)
    concat = lax.all_to_all(branch_out, "branch", split_axis=1, concat_axis=2, tiled=True)
    own_rows = own_hidden.astype(jnp.float32)
    first_normed, first_factor = normalize(own_rows + (project(concat, mixer_weight) + mixer_bias))
    first_out = (first_normed * first_gain + first_shift).astype(jnp.bfloat16)
    inner_pre = grouped(first_out, inner_weight) + inner_bias
    active = jax.nn.gelu(inner_pre, approximate=False).astype(jnp.bfloat16)
    second_normed, second_factor = normalize(
        first_out.astype(jnp.float32) + (grouped(active, outer_weight) + outer_bias)
    )
    output = (second_normed * second_gain + second_shift).astype(jnp.bfloat16)
    grad_output = cotangent.astype(jnp.float32)
    grad_second_gain = jnp.sum(grad_output * second_normed, axis=(0, 1))
    grad_second_shift = jnp.sum(grad_output, axis=(0, 1))
    grad_second = norm_back(grad_output * second_gain, second_normed, second_factor)
    grad_projected = grad_second.astype(jnp.bfloat16)
    grad_outer_bias = column_sum(grad_projected)
    grad_outer_weight = group_grad(active, grad_projected, GROUPS)
    grad_active = group_back(grad_projected, outer_weight).astype(jnp.bfloat16)
    cumulative = 0.5 * (1.0 + lax.erf(inner_pre * ROOT_HALF))
    density = jnp.exp(-0.5 * inner_pre * inner_pre) * INV_ROOT_TAU
    grad_inner = (grad_active.astype(jnp.float32) * (cumulative + inner_pre * density)).astype(
        jnp.bfloat16
    )
    grad_inner_bias = column_sum(grad_inner)
    grad_inner_weight = group_grad(first_out, grad_inner, GROUPS)
    grad_first = grad_second + group_back(grad_inner, inner_weight)
    grad_first_gain = jnp.sum(grad_first * first_normed, axis=(0, 1))
    grad_first_shift = jnp.sum(grad_first, axis=(0, 1))
    grad_mixed = norm_back(grad_first * first_gain, first_normed, first_factor)
    grad_mixer = grad_mixed.astype(jnp.bfloat16)
    grad_mixer_bias = column_sum(grad_mixer)
    grad_mixer_weight = weight_grad(concat, grad_mixer)
    grad_concat = back_project(grad_mixer, mixer_weight).astype(jnp.bfloat16)
    grad_branch = lax.all_to_all(grad_concat, "branch", split_axis=2, concat_axis=1, tiled=True)
    ones_keep = jnp.ones((1, full_length, 1), jnp.bfloat16)

    def attention_grads():
        return attention_backward(
            hidden,
            bounds,
            grad_branch,
            query_weight,
            query_bias,
            key_weight,
            value_weight,
            value_bias,
            depth_kernel,
            point_bias,
            kernel_weight,
            kernel_bias,
        )

    def kernel_grads():
        return convolution_backward(
            hidden,
            bounds,
            grad_branch,
            ones_keep,
            query_weight,
            query_bias,
            depth_kernel,
            key_weight,
            point_bias,
            kernel_weight,
            kernel_bias,
            value_weight,
            value_bias,
        )

    (
        hidden_part,
        grad_query_weight,
        grad_query_bias,
        grad_keys,
        grad_values,
        grad_value_bias,
        grad_depth,
        grad_point_bias,
        grad_kernel,
        grad_kernel_bias,
    ) = lax.cond(branch_side == 0, attention_grads, kernel_grads)
    hidden_grad = (
        lax.psum_scatter(
            hidden_part.astype(jnp.bfloat16), "branch", scatter_dimension=1, tiled=True
        ).astype(jnp.float32)
        + grad_mixed
    )
    shared = lax.psum(
        (
            grad_query_weight,
            grad_query_bias,
            grad_mixer_weight,
            grad_mixer_bias,
            grad_first_gain,
            grad_first_shift,
            grad_inner_weight,
            grad_inner_bias,
            grad_outer_weight,
            grad_outer_bias,
            grad_second_gain,
            grad_second_shift,
            grad_depth,
            grad_point_bias,
            grad_kernel,
            grad_kernel_bias,
        ),
        ("branch", "dp"),
    )
    owned = lax.psum((grad_keys[None], grad_values[None], grad_value_bias[None]), "dp")
    return (
        output,
        hidden_grad,
        shared[0],
        shared[1],
        owned[0],
        owned[1],
        owned[2],
        shared[12],
        shared[13],
        shared[14],
        shared[15],
        shared[2],
        shared[3],
        shared[4],
        shared[5],
        shared[6],
        shared[7],
        shared[8],
        shared[9],
        shared[10],
        shared[11],
    )


def solution(mesh):
    return jax.shard_map(
        shards,
        mesh=mesh,
        in_specs=(
            P("dp", None, None),
            P("dp", None),
            P(),
            P(),
            P("branch", None, None),
            P("branch", None, None),
            P("branch", None),
            P(),
            P(),
            P(),
            P(),
            P(),
            P(),
            P(),
            P(),
            P(),
            P(),
            P(),
            P(),
            P(),
            P(),
            P("dp", "branch", None),
        ),
        out_specs=(
            P("dp", "branch", None),
            P("dp", "branch", None),
            P(),
            P(),
            P("branch", None, None),
            P("branch", None, None),
            P("branch", None),
            P(),
            P(),
            P(),
            P(),
            P(),
            P(),
            P(),
            P(),
            P(),
            P(),
            P(),
            P(),
            P(),
            P(),
        ),
        check_vma=False,
    )
```

profile of v0, /device:TPU:0, one launch (start us, length us, event | category | flops | bytes accessed | tf_op | source)
XLA Modules:
  0.0 723.6 jit_solution(16527274530538020231)
XLA Ops:
  8.0 39.3 %conditional.2 = (bf16[4,512,384]{1,2,0:T(8,128)(2,1)}) conditional(s32[]{:T(128)} %convert_element_type.369, (s32[4,2]{0,1:T(2,128)}, bf16[4,512,768]{2,1,0:T(8,128)(2,1)}, f32[9,768]{1,0:T(8,128)}, bf16[768,384]{1,0:T(8,128)(2,1)}, f32[384]{0:T(512)}, /*index=5*/bf16[768,384]{1,0:T(8,128)(2,1)}, f32[384]{0:T(512)}, bf16[384,54]{0,1:T(8,128)(2,1)}, ...), branch_computations={%region_0.3_spmd, %region_3.6_spmd} | conditional | flops 5276174848 | bytes 89964712 | solution.py:452
  19.8 15.4 %fusion.191 = (f32[4,6,512]{2,1,0:T(8,128)S(1)}, f32[4,6,512,512]{2,3,1,0:T(8,128)}) fusion(pred[4,512]{1,0:T(4,128)(4,1)S(1)} %iota_compare_fusion.2, bf16[4,512,6,64]{1,3,2,0:T(8,128)(2,1)} %bitcast.454, bf16[4,512,6,64]{1,3,2,0:T(8,128)(2,1)} %bitcast.453), kind=kOutput, calls=%fused_computation.441 | convolution fusion | flops 830472704 | bytes 28362752 | tf_op jit(solution)/shard_map/cond/branch_1_fun/sub | solution.py:68
  35.2 12.1 %fusion.26 = bf16[4,6,64,512]{3,2,1,0:T(8,128)(2,1)} fusion(bf16[4,512,6,64]{1,3,2,0:T(8,128)(2,1)} %bitcast.452, f32[4,6,512,512]{2,3,1,0:T(8,128)} %get-tuple-element.332, f32[4,6,512]{2,1,0:T(8,128)S(1)} %get-tuple-element.331), kind=kOutput, calls=%fused_computation.86 | convolution fusion | flops 817889280 | bytes 28360704 | tf_op jit(solution)/shard_map/cond/branch_1_fun/rhqk,rkhe->rqhe/dot_general | solution.py:123
  51.1 5.5 all-to-all-start
  57.0 20.8 %all-to-all-done = bf16[4,512,384]{2,0,1:T(4,128)(2,1)} async-done(((bf16[4,512,384]{2,0,1:T(4,128)(2,1)}), bf16[4,512,384]{2,0,1:T(4,128)(2,1)}, u32[]{:S(2)}, u32[]{:S(2)}) %all-to-all-start) | async-done | bytes 1572896 | tf_op jit(solution)/shard_map/all_to_all | solution.py:453
  82.0 4.9 all_to_all.29
  98.4 4.9 copy.224
  103.3 33.0 %fusion.133 = (bf16[4,256,2,1536]{3,1,0,2:T(8,128)(2,1)S(1)}, f32[2,4,256,1536]{3,2,1,0:T(8,128)}) fusion(f32[2,1536]{1,0:T(2,128)S(1)} %add.416, bf16[4,256,2,384]{1,3,0,2:T(8,128)(2,1)} %copy.224, bf16[2,384,1536]{2,1,0:T(8,128)(2,1)S(1)} %copy-done), kind=kOutput, calls=%fused_computation.353 | convolution fusion | flops 2623537152 | bytes 22818816 | tf_op jit(solution)/shard_map/rsgi,gio->rsgo/dot_general | solution.py:44
  150.5 12.0 %convert_reduce_fusion.6 = (f32[2,1536]{1,0:T(2,128)}, bf16[4,256,2,1536]{3,1,0,2:T(8,128)(2,1)S(1)}) fusion(f32[2,4,256,1536]{3,2,1,0:T(8,128)} %get-tuple-element.377, f32[2,1536]{1,0:T(2,128)S(1)} %add.416, bf16[2,1536,384]{2,1,0:T(8,128)(2,1)S(1)} %copy-done.88, bf16[4,32,2,8,384]{4,3,2,1,0:T(8,128)(2,1)S(1)} %bitcast.435), kind=kOutput, calls=%fused_computation.367 | convolution fusion | flops 2463101952 | bytes 22831104 | tf_op jit(solution)/shard_map/rsgo,gio->rsgi/dot_general | solution.py:61
  179.2 21.7 %all_to_all.36 = bf16[4,256,768]{1,0,2:T(4,128)(2,1)S(1)} all-to-all(bf16[4,256,768]{1,0,2:T(4,128)(2,1)S(1)} %copy.219), channel_id=1, replica_groups=mesh['branch'=2,'dp'=16] {'branch'}, dimensions={2} | all-to-all | bytes 3145728 | tf_op jit(solution)/shard_map/all_to_all | solution.py:486
  206.6 120.2 %conditional.3 = (bf16[4,512,768]{2,1,0:T(8,128)(2,1)}, f32[768,384]{0,1:T(8,128)}, f32[384]{0:T(512)}, f32[768,384]{1,0:T(8,128)S(1)}, f32[768,384]{0,1:T(8,128...) conditional(s32[]{:T(128)} %convert_element_type.369, ...), branch_computations={%region_14.40_spmd, %region_40.46_spmd} | conditional | flops 14995675136 | bytes 333087872 | solution.py:533
  220.6 15.6 %fusion.192 = (f32[4,6,512]{2,1,0:T(8,128)S(1)}, f32[4,6,512,512]{2,3,1,0:T(8,128)}) fusion(pred[4,512]{1,0:T(4,128)(4,1)S(1)} %iota_compare_fusion.5, bf16[4,512,6,64]{1,3,2,0:T(8,128)(2,1)} %bitcast.420, bf16[4,512,6,64]{1,3,2,0:T(8,128)(2,1)} %bitcast.432), kind=kOutput, calls=%fused_computation.442 | convolution fusion | flops 830472704 | bytes 28362752 | tf_op jit(solution)/shard_map/cond/branch_1_fun/sub | solution.py:68
  236.2 11.7 %convert_reduce_fusion.4 = (f32[6,64]{1,0:T(8,128)S(1)}, bf16[4,6,512,64]{2,3,1,0:T(8,128)(2,1)}) fusion(bf16[4,512,6,64]{1,3,2,0:T(8,128)(2,1)S(1)} %bitcast.396, f32[4,6,512,512]{2,3,1,0:T(8,128)} %get-tuple-element.334, f32[4,6,512]{2,1,0:T(8,128)S(1)} %get-tuple-element.333), kind=kOutput, calls=%fused_computation.325 | convolution fusion | flops 820248192 | bytes 28362240 | tf_op jit(solution)/shard_map/cond/branch_1_fun/rhqk,rqhe->rkhe/dot_general | solution.py:150
  252.7 16.8 %fusion.107 = (f32[4,6,512]{2,1,0:T(8,128)S(1)}, f32[4,6,512,512]{3,2,1,0:T(8,128)}) fusion(f32[4,6,512,512]{2,3,1,0:T(8,128)} %get-tuple-element.334, f32[4,6,512]{2,1,0:T(8,128)S(1)} %get-tuple-element.333, bf16[4,512,6,64]{1,3,2,0:T(8,128)(2,1)} %bitcast.451, bf16[4,512,6,64]{1,3,2,0:T(8,128)(2,1)S(1)} %bitcast.397), kind=kOutput, calls=%fused_computation.312 | convolution fusion | flops 824168448 | bytes 53575680 | tf_op jit(solution)/shard_map/cond/branch_1_fun/rqhe,rkhe->rhqk/dot_general | solution.py:156
  269.5 21.4 %fusion.109 = bf16[4,6,512,512]{2,3,1,0:T(8,128)(2,1)} fusion(f32[4,6,512,512]{3,2,1,0:T(8,128)} %get-tuple-element.336, f32[4,6,512]{2,1,0:T(8,128)S(1)} %get-tuple-element.335, f32[4,6,512,512]{2,3,1,0:T(8,128)} %get-tuple-element.334, f32[4,6,512]{2,1,0:T(8,128)S(1)} %get-tuple-element.333), kind=kLoop, calls=%fused_computation.314 | loop fusion | flops 25165824 | bytes 63012864 | tf_op jit(solution)/shard_map/cond/branch_1_fun/convert_element_type | solution.py:162
  290.9 8.6 %multiply_convert_fusion.4 = bf16[4,6,64,512]{3,2,1,0:T(8,128)(2,1)S(1)} fusion(bf16[4,512,6,64]{1,3,2,0:T(8,128)(2,1)S(1)} %bitcast.421, bf16[4,6,512,512]{2,3,1,0:T(8,128)(2,1)} %fusion.109), kind=kOutput, calls=%fused_computation.327 | convolution fusion | flops 806879232 | bytes 15728640 | tf_op jit(solution)/shard_map/cond/branch_1_fun/rhqk,rqhe->rkhe/dot_general | solution.py:169
  299.5 7.8 %convert_reduce_fusion.5 = (f32[6,64]{1,0:T(8,128)S(1)}, bf16[4,6,64,512]{3,2,1,0:T(8,128)(2,1)}) fusion(bf16[4,512,6,64]{1,3,2,0:T(8,128)(2,1)S(1)} %bitcast.433, bf16[4,6,512,512]{2,3,1,0:T(8,128)(2,1)} %fusion.109), kind=kOutput, calls=%fused_computation.326 | convolution fusion | flops 808451712 | bytes 15730176 | tf_op jit(solution)/shard_map/cond/branch_1_fun/rhqk,rkhe->rqhe/dot_general | solution.py:164
  308.0 4.9 convolution_bitcast_fusion.6
  335.9 8.6 %convolution_bitcast_fusion.7 = f32[2,1536,384]{2,1,0:T(8,128)} fusion(bf16[4,256,2,1536]{3,1,0,2:T(8,128)(2,1)} %copy-done.94, bf16[4,32,2,8,384]{4,3,2,1,0:T(8,128)(2,1)S(1)} %bitcast.436), kind=kOutput, calls=%fused_computation.390 | convolution fusion | flops 2415919104 | bytes 12582912 | tf_op jit(solution)/shard_map/rsgi,rsgo->gio/dot_general | solution.py:53
  344.5 7.1 convolution_bitcast_fusion.8
  353.9 62.5 %all-reduce.22 = (f32[384]{0:T(512)}, f32[9,768]{1,0:T(8,128)}, f32[384]{0:T(512)}, f32[54]{0:T(128)}, f32[768]{0:T(1024)}, /*index=5*/f32[768]{0:T(1024)}, f32[...) all-reduce(f32[384]{0:T(512)S(1)} %copy-done.80, ...), channel_id=1, replica_groups=mesh['branch'=2,'dp'=16] {'branch','dp'}, use_global_device_ids=true, to_apply=%region_48.49 | all-reduce | flops 15414 | bytes 123312 | tf_op jit(solution)/shard_map/psum | solution.py:540
  416.4 31.6 %psum.137 = f32[1,384]{1,0:T(1,128)} all-reduce(f32[1,384]{1,0:T(1,128)S(1)} %broadcast_in_dim.117), channel_id=1, replica_groups=mesh['branch'=2,'dp'=16] {'dp'}, use_global_device_ids=true, to_apply=%region_51.52 | all-reduce | flops 384 | bytes 3072 | tf_op jit(solution)/shard_map/psum | solution.py:561
  448.1 5.1 convert_add_fusion
  456.5 246.8 %all-reduce.28.cloned.1.call-done = (f32[768,384]{1,0:T(8,128)}, f32[384,54]{0,1:T(8,128)}, f32[768,768]{1,0:T(8,128)}, f32[2,384,1536]{2,1,0:T(8,128)}, f32[2,1536,384]{2,1,0:T(8,128)}) async-done(((f32[768,384]{1,0:T(8,128)}, f32[384,54]{0,1:T(8,128)}, f32[768,768]{1,0:T(8,128)}, f32[2,384,1536]{2,1,0:T(8,128)}, f32[2,1536,384]{2,1,0:T(8,128)}), (f32[768,384]{1,0:T(8,128)}, f32[384,54]{0,1:T(8,128)}, ...) | async-done | bytes 13059088 | tf_op jit(solution)/shard_map/psum | solution.py:540
  (223 shorter events, 123.9 us)
Async XLA Ops:
  8.0 95.3 %copy-start = (bf16[2,384,1536]{2,1,0:T(8,128)(2,1)S(1)}, bf16[2,384,1536]{2,1,0:T(8,128)(2,1)}, u32[]{:S(2)}) copy-start(bf16[2,384,1536]{2,1,0:T(8,128)(2,1)} %param.41) | copy-start | bytes 7077892
  47.3 9.7 %copy-start.76 = (f32[3072]{0:T(1024)S(1)}, f32[3072]{0:T(1024)}, u32[]{:S(2)}) copy-start(f32[3072]{0:T(1024)} %param.42) | copy-start | bytes 36868
  51.1 26.7 %all-to-all-start = ((bf16[4,512,384]{2,0,1:T(4,128)(2,1)}), bf16[4,512,384]{2,0,1:T(4,128)(2,1)}, u32[]{:S(2)}, u32[]{:S(2)}) async-start(bf16[4,512,384]{2,0,1:T(4,128)(2,1)} %copy.213), calls=%async_computation | async-start | bytes 3145728 | tf_op jit(solution)/shard_map/all_to_all | solution.py:453
  56.6 391.4 %reduce-scatter.2.cloned.1.call-start = ((), (), s32[]{:S(2)}) async-start(), calls=%async_computation.3 | async-start | bytes 4718592 | tf_op jit(solution)/shard_map/reduce_scatter | solution.py:535
  77.8 9.1 %copy-start.90 = (f32[768]{0:T(1024)S(1)}, f32[768]{0:T(1024)}, u32[]{:S(2)}) copy-start(f32[768]{0:T(1024)} %param.38) | copy-start | bytes 9220
  90.7 80.4 %copy-start.48 = (f32[4,256]{1,0:T(4,128)}, f32[4,256]{1,0:T(4,128)S(1)}, u32[]{:S(2)}) copy-start(f32[4,256]{1,0:T(4,128)S(1)} %broadcast_multiply_fusion.5) | copy-start | bytes 12292
  92.3 78.8 %copy-start.53 = (f32[4,256]{1,0:T(4,128)}, f32[4,256]{1,0:T(4,128)S(1)}, u32[]{:S(2)}) copy-start(f32[4,256]{1,0:T(4,128)S(1)} %add_rsqrt_fusion.1) | copy-start | bytes 12292
  103.3 35.6 %copy-start.88 = (bf16[2,1536,384]{2,1,0:T(8,128)(2,1)S(1)}, bf16[2,1536,384]{2,1,0:T(8,128)(2,1)}, u32[]{:S(2)}) copy-start(bf16[2,1536,384]{2,1,0:T(8,128)(2,1)} %param.43) | copy-start | bytes 7077892
  150.5 12.1 %copy-start.37 = (bf16[4,256,768]{2,1,0:T(8,128)(2,1)}, bf16[4,256,768]{2,1,0:T(8,128)(2,1)S(1)}, u32[]{:S(2)}) copy-start(bf16[4,256,768]{2,1,0:T(8,128)(2,1)S(1)} %get-tuple-element.314) | copy-start | bytes 4718596
  210.5 7.5 %copy-start.46 = (bf16[768,384]{1,0:T(8,128)(2,1)}, bf16[768,384]{1,0:T(8,128)(2,1)S(1)}, u32[]{:S(2)}) copy-start(bf16[768,384]{1,0:T(8,128)(2,1)S(1)} %get-tuple-element.111) | copy-start | bytes 1769476 | tf_op jit(solution)/shard_map/cond
  269.5 21.4 %copy-start.20 = (bf16[4,512,384]{1,2,0:T(8,128)(2,1)S(1)}, bf16[4,512,384]{1,2,0:T(8,128)(2,1)}, u32[]{:S(2)}) copy-start(bf16[4,512,384]{1,2,0:T(8,128)(2,1)} %add_convert_fusion.15) | copy-start | bytes 4718596 | tf_op jit(solution)/shard_map/cond
  290.9 8.6 %copy-start.34 = (bf16[4,512,384]{1,2,0:T(8,128)(2,1)S(1)}, bf16[4,512,384]{1,2,0:T(8,128)(2,1)}, u32[]{:S(2)}) copy-start(bf16[4,512,384]{1,2,0:T(8,128)(2,1)} %convolution_convert_fusion.3) | copy-start | bytes 4718596 | tf_op jit(solution)/shard_map/cond
  326.9 6.1 copy-start.17
  326.9 6.1 copy-start.47
  327.0 129.5 %all-reduce.30.cloned.1.call-start = ((), (), s32[]{:S(2)}) async-start(), calls=%async_computation.5 | async-start | bytes 4718592 | tf_op jit(solution)/shard_map/psum | solution.py:561
  335.8 367.4 %all-reduce.28.cloned.1.call-start = ((), (), s32[]{:S(2)}) async-start(), calls=%async_computation.4 | async-start | bytes 26124288 | tf_op jit(solution)/shard_map/psum | solution.py:540
  335.9 8.6 %copy-start.35 = (bf16[4,256,2,384]{1,3,0,2:T(8,128)(2,1)S(1)}, bf16[4,256,2,384]{1,3,0,2:T(8,128)(2,1)}, u32[]{:S(2)}) copy-start(bf16[4,256,2,384]{1,3,0,2:T(8,128)(2,1)} %copy.224) | copy-start | bytes 4718596
  344.5 7.1 copy-start.19
  353.0 95.0 %copy-start.49 = (f32[4,256]{1,0:T(4,128)S(1)}, f32[4,256]{1,0:T(4,128)}, u32[]{:S(2)}) copy-start(f32[4,256]{1,0:T(4,128)} %copy-done.48) | copy-start | bytes 12292
  353.1 95.0 %copy-start.54 = (f32[4,256]{1,0:T(4,128)S(1)}, f32[4,256]{1,0:T(4,128)}, u32[]{:S(2)}) copy-start(f32[4,256]{1,0:T(4,128)} %copy-done.53) | copy-start | bytes 12292
  353.1 95.0 %copy-start.56 = (f32[768]{0:T(1024)S(1)}, f32[768]{0:T(1024)}, u32[]{:S(2)}) copy-start(f32[768]{0:T(1024)} %param.39) | copy-start | bytes 9220
  353.1 95.0 %copy-start.60 = (f32[4,256]{1,0:T(4,128)S(1)}, f32[4,256]{1,0:T(4,128)}, u32[]{:S(2)}) copy-start(f32[4,256]{1,0:T(4,128)} %copy-done.59) | copy-start | bytes 12292
  353.1 95.0 %copy-start.62 = (f32[4,256]{1,0:T(4,128)S(1)}, f32[4,256]{1,0:T(4,128)}, u32[]{:S(2)}) copy-start(f32[4,256]{1,0:T(4,128)} %copy-done.61) | copy-start | bytes 12292
  456.5 250.3 %copy-start.40 = (f32[1,768,384]{2,1,0:T(8,128)S(1)}, f32[1,768,384]{2,1,0:T(8,128)}, u32[]{:S(2)}) copy-start(f32[1,768,384]{2,1,0:T(8,128)} %get-tuple-element.407) | copy-start | bytes 3538948
  (55 other events, 163.9 us)
Sparse Core Ops, SparseCore 0:
  327.1 64.5 reduce-scatter.1
Sparse Core Ops, SparseCore 1:
  335.9 120.5 all-reduce.29
  465.6 237.6 all-reduce.27
where the time goes:
time: 731 us; the launch traced here: 724 us
  waiting for transfers between devices  271 us (37%)
  matrix products  206 us (28%)
  blocking collectives  116 us (16%)
  local copies, waits for them, and re-layouts  62.3 us (9%)
  other arithmetic  41.1 us (6%)
  between operations  16.5 us (2%)
    psum x1, waiting for transfers between devices, shards(): lax.psum((grad_query_weight, grad_query_bias, grad_mixer_weight, grad_mix...  247 us
    psum x1, blocking collectives, shards(): lax.psum((grad_query_weight, grad_query_bias, grad_mixer_weight, grad_mix...  62.5 us
    dot_general x2, matrix products, grouped(): jnp.einsum('rsgi,gio->rsgo', split_source, matrix, preferred_element_type...  36.4 us
    psum x1, blocking collectives, shards(): lax.psum((grad_keys[None], grad_values[None], grad_value_bias[None]), 'dp')  31.6 us
    sub x2, matrix products, softmax_last(): raised = jnp.exp(scores - row_peak)  31 us
    dot_general x7, matrix products, project(): jnp.einsum('rsd,de->rse', source, matrix, preferred_element_type=jnp.floa...  23.7 us
    unnamed x131, local copies, waits for them, and re-layouts  22.9 us
    all_to_all x1, blocking collectives, shards(): lax.all_to_all(grad_concat, 'branch', split_axis=2, concat_axis=1, tiled=...  21.7 us
  transfers between devices with their start and end apart: 4, of which 3 were waited for; matrix products, arithmetic and copies ran while one was open for 4% of the time, Pallas kernels for 0%

commit v1 on v0

v1 whole, which is shorter than its diff:
```python
import functools

import jax
import jax.numpy as jnp
import numpy as np
from jax import lax
from jax.experimental import pallas as pl
from jax.experimental.pallas import tpu as pltpu
from jax.sharding import PartitionSpec as P

HEADS = 6
HEAD_SIZE = 64
KERNEL = 9
RADIUS = KERNEL // 2
SLAB = 8
LANES = 128
PAD = 8

NEGATIVE = -1000000000.0
EPSILON = 1e-05
INV_ROOT_TAU = 0.3989422804014327
TAIL_SLOPE = 0.36
TAIL_TERMS = (
    0.14361732768142335,
    0.14369104425682297,
    0.12391285318517967,
    0.09656500864495021,
    -0.002026438221833662,
    0.11038580625572408,
    -0.22684055188970365,
    0.1413848307004008,
    -0.030689918446024287,
)

BF = jnp.bfloat16
F32 = jnp.float32
VMEM_LIMIT = 62 * 1024 * 1024


def mm(left, right):
    return jnp.dot(left, right, preferred_element_type=F32)


def mm_nt(left, right):
    return lax.dot_general(left, right, (((1,), (1,)), ((), ())), preferred_element_type=F32)


def rowsum(value):
    return jnp.sum(value, axis=0, keepdims=True)


def fill_strips(strips_ref, value, length):
    strips = strips_ref.shape[0]
    zero = jnp.zeros((PAD, LANES), F32)
    for strip in range(strips):
        strips_ref[strip, 0:PAD, :] = zero
        strips_ref[strip, PAD + length : 2 * PAD + length, :] = zero
        strips_ref[strip, PAD : PAD + length, :] = value[
            :, strip * LANES : (strip + 1) * LANES
        ].astype(F32)


def head_pair_rows(rows, head):
    own = rows[head * HEAD_SIZE : (head + 1) * HEAD_SIZE, :]
    zero = jnp.zeros_like(own)
    return jnp.concatenate([own, zero] if head % 2 == 0 else [zero, own], axis=0)


def forward_kernel(
    place,
    bounds,
    x_ref,
    wq_ref,
    bq_ref,
    wa_ref,
    wb_ref,
    bb_ref,
    depth_ref,
    pb_ref,
    kwt_ref,
    kb_ref,
    spread_ref,
    *rest,
):
    (
        cat_ref,
        q_ref,
        k_ref,
        v_ref,
        probs_ref,
        att_t_ref,
        dm_ref,
        kc_ref,
        cq_ref,
        joint_ref,
        taps_ref,
        vc_ref,
        qt_s,
        vt_s,
        xs_s,
        vs_s,
        tw_s,
        wide_s,
    ) = rest[-18:]
    row = place[0] + pl.program_id(0)
    first_end = bounds[row, 0]
    valid = bounds[row, 1]
    length = x_ref.shape[1]
    x = x_ref[0]
    queries = (mm(x, wq_ref[...]) + bq_ref[...]).astype(BF)

    @pl.when(place[1] == 1)
    def _():
        scaled = (queries.astype(F32) * (HEAD_SIZE**-0.5)).astype(BF)
        q_ref[0] = scaled
        qt_s[...] = scaled.T
        k_ref[0] = mm(x, wa_ref[...]).astype(BF)
        v = (mm(x, wb_ref[...]) + bb_ref[...]).astype(BF)
        v_ref[0] = v
        vt_s[...] = v.T
        seen = lax.broadcasted_iota(jnp.int32, (length, 1), 0) < valid
        for head in range(HEADS):
            pair = head // 2
            keys = k_ref[0, :, pair * LANES : (pair + 1) * LANES]
            scores = mm(keys, head_pair_rows(qt_s, head))
            scores = jnp.where(seen, scores, NEGATIVE)
            raised = jnp.exp(scores - jnp.max(scores, axis=0, keepdims=True))
            probs = (raised * (1.0 / rowsum(raised))).astype(BF)
            probs_ref[0, head] = probs
            span = slice(head * HEAD_SIZE, (head + 1) * HEAD_SIZE)
            att_t_ref[0, span, :] = mm(vt_s[span, :], probs).astype(BF)
        cat_ref[0] = att_t_ref[0].T

    @pl.when(place[1] == 0)
    def _():
        fill_strips(xs_s, x, length)
        piece = LANES
        for strip in range(xs_s.shape[0]):
            lanes = slice(strip * LANES, (strip + 1) * LANES)
            for at in range(0, length, piece):
                total = None
                for tap in range(KERNEL):
                    begin = PAD - RADIUS + tap + at
                    term = xs_s[strip, begin : begin + piece, :] * depth_ref[tap : tap + 1, lanes]
                    total = term if total is None else total + term
                dm_ref[0, at : at + piece, lanes] = total.astype(BF)
        key_conv = mm(dm_ref[0], wa_ref[...]) + pb_ref[...]
        kc_ref[0] = key_conv
        cq_ref[0] = queries
        joint = (key_conv * queries.astype(F32)).astype(BF)
        joint_ref[0] = joint
        logits = mm_nt(kwt_ref[...], joint) + kb_ref[:, 0:1]
        here = lax.broadcasted_iota(jnp.int32, (SLAB, length), 1)

        def segment(position):
            return jnp.where(position <= first_end, 0, jnp.where(position < valid, 1, 2))

        own_segment = segment(here)
        slabs = []
        for tap in range(KERNEL):
            other = here + (tap - RADIUS)
            same = (other >= 0) & (other < length) & (segment(other) == own_segment)
            slabs.append(jnp.where(same, logits[tap * SLAB : (tap + 1) * SLAB], NEGATIVE))
        peak = functools.reduce(jnp.maximum, slabs)
        slabs = [jnp.exp(slab - peak) for slab in slabs]
        inverse = 1.0 / functools.reduce(jnp.add, slabs)
        for tap in range(KERNEL):
            tw_s[tap * SLAB : (tap + 1) * SLAB, :] = slabs[tap] * inverse
        tw_s[KERNEL * SLAB :, :] = jnp.zeros((LANES - KERNEL * SLAB, length), F32)
        taps_ref[0] = tw_s[...]
        taps = tw_s[...].T
        high = taps.astype(BF)
        low = (taps - high.astype(F32)).astype(BF)
        both = jnp.concatenate([high, low], axis=1)
        width = HEADS * HEAD_SIZE
        for tap in range(KERNEL):
            cols = slice(tap * width, (tap + 1) * width)
            wide_s[:, cols] = mm(both, spread_ref[:, cols])
        vc = (mm(x, wb_ref[...]) + bb_ref[...]).astype(BF)
        vc_ref[0] = vc
        fill_strips(vs_s, vc, length)
        for strip in range(vs_s.shape[0]):
            for at in range(0, length, piece):
                total = None
                for tap in range(KERNEL):
                    begin = PAD - RADIUS + tap + at
                    col = tap * width + strip * LANES
                    term = (
                        vs_s[strip, begin : begin + piece, :]
                        * wide_s[at : at + piece, col : col + LANES]
                    )
                    total = term if total is None else total + term
                cat_ref[0, at : at + piece, strip * LANES : (strip + 1) * LANES] = total.astype(BF)


def spread_table():
    table = np.zeros((2 * LANES, KERNEL, HEADS, HEAD_SIZE), np.float32)
    for tap in range(KERNEL):
        for head in range(HEADS):
            table[tap * SLAB + head, tap, head, :] = 1
            table[LANES + tap * SLAB + head, tap, head, :] = 1
    return jnp.asarray(table.reshape(2 * LANES, -1), BF)


def gather_table():
    table = np.zeros((KERNEL, HEADS, HEAD_SIZE, LANES), np.float32)
    for tap in range(KERNEL):
        for head in range(HEADS):
            table[tap, head, :, tap * SLAB + head] = 1
    return jnp.asarray(table.reshape(-1, LANES), BF)


def whole(array):
    rank = array.ndim
    return pl.BlockSpec(array.shape, lambda *_: (0,) * rank)


def forward(place, bounds, hidden, weights, rows, before=None):
    length, features = hidden.shape[1:]
    width = HEADS * HEAD_SIZE
    spare = rows

    def att_row(r, place, bounds):
        return jnp.where(place[1] == 1, r, spare)

    def conv_row(r, place, bounds):
        return jnp.where(place[1] == 0, r, spare)

    def saved(row_of, shape, dtype):
        zeros = (0,) * len(shape)
        return (
            jax.ShapeDtypeStruct((rows + 1,) + shape, dtype),
            pl.BlockSpec((1,) + shape, lambda r, p, b: (row_of(r, p, b),) + zeros),
        )

    outs = [
        (
            jax.ShapeDtypeStruct((rows, length, 2 * width), BF),
            pl.BlockSpec((1, length, width), lambda r, p, b: (r, 0, 1 - p[1])),
        ),
        saved(att_row, (length, width), BF),
        saved(att_row, (length, width), BF),
        saved(att_row, (length, width), BF),
        saved(att_row, (HEADS, length, length), BF),
        saved(att_row, (width, length), BF),
        saved(conv_row, (length, features), BF),
        saved(conv_row, (length, width), F32),
        saved(conv_row, (length, width), BF),
        saved(conv_row, (length, width), BF),
        saved(conv_row, (LANES, length), F32),
        saved(conv_row, (length, width), BF),
    ]
    in_specs = [pl.BlockSpec((1, length, features), lambda r, p, b: (p[0] + r, 0, 0))]
    in_specs += [whole(w) for w in weights]
    args = [place, bounds, hidden, *weights]
    aliases = {}
    if before is not None:
        aliases = {len(args) + i: i for i in range(len(before))}
        in_specs += [pl.BlockSpec(memory_space=pl.ANY)] * len(before)
        args += list(before)
    return pl.pallas_call(
        forward_kernel,
        out_shape=[o[0] for o in outs],
        grid_spec=pltpu.PrefetchScalarGridSpec(
            num_scalar_prefetch=2,
            grid=(rows,),
            in_specs=in_specs,
            out_specs=[o[1] for o in outs],
            scratch_shapes=[
                pltpu.VMEM((width, length), BF),
                pltpu.VMEM((width, length), BF),
                pltpu.VMEM((features // LANES, length + 2 * PAD, LANES), F32),
                pltpu.VMEM((width // LANES, length + 2 * PAD, LANES), F32),
                pltpu.VMEM((LANES, length), F32),
                pltpu.VMEM((length, KERNEL * width), F32),
            ],
        ),
        input_output_aliases=aliases,
        compiler_params=pltpu.CompilerParams(vmem_limit_bytes=VMEM_LIMIT),
        name="branch_forward",
    )(*args)


def norm(value):
    center = value - jnp.mean(value, axis=-1, keepdims=True)
    factor = lax.rsqrt(jnp.mean(center * center, axis=-1, keepdims=True) + EPSILON)
    return center * factor, factor


def norm_back(gradient, normed, factor):
    return factor * (
        gradient
        - jnp.mean(gradient, axis=-1, keepdims=True)
        - normed * jnp.mean(gradient * normed, axis=-1, keepdims=True)
    )


def middle_kernel(
    place,
    x_ref,
    cat_ref,
    cot_own_ref,
    cot_got_ref,
    mw_ref,
    mb_ref,
    g1_ref,
    b1_ref,
    iw_ref,
    ib_ref,
    ow_ref,
    ob_ref,
    g2_ref,
    b2_ref,
    own_ref,
    send_ref,
    dcat_ref,
    datt_ref,
    dmix_ref,
    grad_ref,
    vec_ref,
    acc_i,
    acc_o,
    acc_m,
    act_s,
    slope_s,
    din_s,
):
    step = pl.program_id(0)
    half = step % 2
    mine = half == place[1]
    features = x_ref.shape[2]
    groups, width, inner = iw_ref.shape
    piece = 512

    @pl.when(step == 0)
    def _():
        acc_i[...] = jnp.zeros_like(acc_i)
        acc_o[...] = jnp.zeros_like(acc_o)
        acc_m[...] = jnp.zeros_like(acc_m)
        vec_ref[...] = jnp.zeros_like(vec_ref)

    cat = cat_ref[0]
    normed1, factor1 = norm(x_ref[0].astype(F32) + (mm(cat, mw_ref[...]) + mb_ref[...]))
    first = (normed1 * g1_ref[...] + b1_ref[...]).astype(BF)
    projected = []
    for g in range(groups):
        part = first[:, g * width : (g + 1) * width]
        for at in range(0, inner, piece):
            lanes = slice(g * inner + at, g * inner + at + piece)
            pre = mm(part, iw_ref[g, :, at : at + piece]) + ib_ref[:, lanes]
            bell = jnp.exp(-0.5 * pre * pre)
            t = 1.0 / (1.0 + TAIL_SLOPE * jnp.abs(pre))
            tail = jnp.full_like(t, TAIL_TERMS[-1])
            for term in TAIL_TERMS[-2::-1]:
                tail = tail * t + term
            tail = bell * (t * tail)
            phi = jnp.where(pre >= 0, 1.0 - tail, tail)
            act_s[:, lanes] = (pre * phi).astype(BF)
            slope_s[:, lanes] = phi + pre * (bell * INV_ROOT_TAU)
        projected.append(mm(act_s[:, g * inner : (g + 1) * inner], ow_ref[g]))
    projected = jnp.concatenate(projected, axis=1)
    normed2, factor2 = norm(first.astype(F32) + (projected + ob_ref[...]))
    output = (normed2 * g2_ref[...] + b2_ref[...]).astype(BF)

    @pl.when(mine)
    def _():
        own_ref[0] = output

    @pl.when(jnp.logical_not(mine))
    def _():
        send_ref[0] = output

    cot = jnp.where(mine, cot_own_ref[0].astype(F32), cot_got_ref[0].astype(F32))
    dsecond = norm_back(cot * g2_ref[...], normed2, factor2)
    dproj = dsecond.astype(BF)
    vec_ref[1:2, 3 * features : 4 * features] += rowsum(dproj.astype(F32))
    vec_ref[2:3, 0:features] += rowsum(cot * normed2)
    vec_ref[2:3, features : 2 * features] += rowsum(cot)
    dfirst = []
    for g in range(groups):
        cols = slice(g * width, (g + 1) * width)
        dpart = dproj[:, cols]
        for at in range(0, inner, piece):
            lanes = slice(g * inner + at, g * inner + at + piece)
            dact = mm_nt(dpart, ow_ref[g, at : at + piece, :]).astype(BF)
            din = (dact.astype(F32) * slope_s[:, lanes]).astype(BF)
            din_s[:, lanes] = din
            vec_ref[0:1, lanes] += rowsum(din.astype(F32))
        group = slice(g * inner, (g + 1) * inner)
        acc_o[g] += mm(dpart.T, act_s[:, group])
        acc_i[g] += mm(first[:, cols].T, din_s[:, group])
        dfirst.append(dsecond[:, cols] + mm_nt(din_s[:, group], iw_ref[g]))
    dfirst = jnp.concatenate(dfirst, axis=1)
    vec_ref[1:2, features : 2 * features] += rowsum(dfirst * normed1)
    vec_ref[1:2, 2 * features : 3 * features] += rowsum(dfirst)
    dmixed = norm_back(dfirst * g1_ref[...], normed1, factor1)
    dmix_ref[0] = dmixed
    dmixer = dmixed.astype(BF)
    vec_ref[1:2, 0:features] += rowsum(dmixer.astype(F32))
    acc_m[...] += mm(cat.T, dmixer)
    dcat_ref[0] = mm_nt(dmixer, mw_ref[...]).astype(BF)
    datt_ref[0] = mm_nt(mw_ref[0:width, :], dmixer).astype(BF)

    @pl.when(step == pl.num_programs(0) - 1)
    def _():
        for g in range(groups):
            grad_ref[g * width : (g + 1) * width, :] = acc_i[g].astype(BF)
            grad_ref[(groups + g) * width : (groups + g + 1) * width, :] = acc_o[g].astype(BF)
        grad_ref[2 * groups * width :, 0:features] = acc_m[0:width, :].astype(BF)
        grad_ref[2 * groups * width :, features:] = acc_m[width:, :].astype(BF)


def middle(place, hidden, cat, cot_own, cot_got, weights, rows):
    length, features = hidden.shape[1:]
    half = length // 2
    groups, width, inner = weights[4].shape

    def per_chunk(shape, dtype):
        return (
            jax.ShapeDtypeStruct((rows, length, shape), dtype),
            pl.BlockSpec((1, half, shape), lambda s, p: (s // 2, s % 2, 0)),
        )

    per_row = (
        jax.ShapeDtypeStruct((rows, half, features), BF),
        pl.BlockSpec((1, half, features), lambda s, p: (s // 2, 0, 0)),
    )
    outs = [
        per_row,
        per_row,
        per_chunk(features, BF),
        (
            jax.ShapeDtypeStruct((rows, width, length), BF),
            pl.BlockSpec((1, width, half), lambda s, p: (s // 2, 0, s % 2)),
        ),
        per_chunk(features, F32),
        (
            jax.ShapeDtypeStruct((5 * width, inner), BF),
            pl.BlockSpec((5 * width, inner), lambda s, p: (0, 0)),
        ),
        (
            jax.ShapeDtypeStruct((SLAB, groups * inner), F32),
            pl.BlockSpec((SLAB, groups * inner), lambda s, p: (0, 0)),
        ),
    ]
    return pl.pallas_call(
        middle_kernel,
        out_shape=[o[0] for o in outs],
        grid_spec=pltpu.PrefetchScalarGridSpec(
            num_scalar_prefetch=1,
            grid=(2 * rows,),
            in_specs=[
                pl.BlockSpec((1, half, features), lambda s, p: (p[0] + s // 2, s % 2, 0)),
                pl.BlockSpec((1, half, features), lambda s, p: (s // 2, s % 2, 0)),
                pl.BlockSpec((1, half, features), lambda s, p: (p[0] + s // 2, 0, 0)),
                pl.BlockSpec((1, half, features), lambda s, p: (s // 2, 0, 0)),
                *[whole(w) for w in weights],
            ],
            out_specs=[o[1] for o in outs],
            scratch_shapes=[
                pltpu.VMEM((groups, width, inner), F32),
                pltpu.VMEM((groups, width, inner), F32),
                pltpu.VMEM((features, features), F32),
                pltpu.VMEM((half, groups * inner), BF),
                pltpu.VMEM((half, groups * inner), F32),
                pltpu.VMEM((half, groups * inner), BF),
            ],
        ),
        compiler_params=pltpu.CompilerParams(vmem_limit_bytes=VMEM_LIMIT),
        name="shared_layers",
    )(place, hidden, cat, cot_own, cot_got, *weights)


def conv_back_kernel(
    place,
    x_ref,
    dcat_ref,
    dmix_ref,
    dm_ref,
    kc_ref,
    q_ref,
    joint_ref,
    taps_ref,
    vc_ref,
    wa_ref,
    wb_ref,
    depth_ref,
    kwt_ref,
    spread_ref,
    collect_ref,
    part_ref,
    dq_ref,
    grad_ref,
    small_ref,
    kgrad_ref,
    vs_s,
    xs_s,
    ys_s,
    ds_s,
    prod_s,
    acc_a,
    acc_b,
):
    step = pl.program_id(0)
    length, features = x_ref.shape[1:]
    width = HEADS * HEAD_SIZE
    piece = LANES

    @pl.when(step == 0)
    def _():
        acc_a[...] = jnp.zeros_like(acc_a)
        acc_b[...] = jnp.zeros_like(acc_b)
        small_ref[...] = jnp.zeros_like(small_ref)
        kgrad_ref[...] = jnp.zeros_like(kgrad_ref)

    x = x_ref[0]
    dconv = dcat_ref[0].astype(F32)
    fill_strips(vs_s, vc_ref[0], length)
    taps_t = taps_ref[0]
    taps = taps_t.T
    high = taps.astype(BF)
    low = (taps - high.astype(F32)).astype(BF)
    both = jnp.concatenate([high, low], axis=1)
    zero = jnp.zeros((PAD, LANES), F32)
    for tap in range(KERNEL):
        spread = mm(both, spread_ref[:, tap * width : (tap + 1) * width])
        for strip in range(width // LANES):
            lanes = slice(strip * LANES, (strip + 1) * LANES)
            begin = PAD - RADIUS + tap
            prod_s[:, tap * width + strip * LANES : tap * width + (strip + 1) * LANES] = (
                dconv[:, lanes] * vs_s[strip, begin : begin + length, :]
            ).astype(BF)
            slot = tap * (width // LANES) + strip
            ys_s[slot, 0:PAD, :] = zero
            ys_s[slot, PAD + length :, :] = zero
            ys_s[slot, PAD : PAD + length, :] = spread[:, lanes] * dconv[:, lanes]
    dvc = []
    for strip in range(width // LANES):
        total = None
        for tap in range(KERNEL):
            begin = PAD + RADIUS - tap
            term = ys_s[tap * (width // LANES) + strip, begin : begin + length, :]
            total = term if total is None else total + term
        dvc.append(total.astype(BF))
    dvc = jnp.concatenate(dvc, axis=1)
    dtaps = mm(prod_s[...], collect_ref[...]).T
    slabs = [dtaps[t * SLAB : (t + 1) * SLAB] for t in range(KERNEL)]
    weights = [taps_t[t * SLAB : (t + 1) * SLAB] for t in range(KERNEL)]
    total = functools.reduce(jnp.add, [a * b for a, b in zip(slabs, weights)])
    slabs = [b * (a - total) for a, b in zip(slabs, weights)]
    slabs.append(jnp.zeros((LANES - KERNEL * SLAB, length), F32))
    dlogits_t = jnp.concatenate(slabs, axis=0)
    dlogits = dlogits_t.T.astype(BF)
    rounded_t = dlogits_t.astype(BF)
    kgrad_ref[:, 0:width] += mm(rounded_t, joint_ref[0])
    kgrad_ref[:, width : width + LANES] += jnp.broadcast_to(
        jnp.sum(rounded_t.astype(F32), axis=1, keepdims=True), (LANES, LANES)
    )
    djoint = mm(dlogits, kwt_ref[...]).astype(BF).astype(F32)
    dkey = (djoint * q_ref[0].astype(F32)).astype(BF)
    dq_ref[0] = (djoint * kc_ref[0]).astype(BF)
    small_ref[9:10, 0:width] += rowsum(dkey.astype(F32))
    small_ref[9:10, width : 2 * width] += rowsum(dvc.astype(F32))
    ddepth = mm_nt(dkey, wa_ref[...]).astype(BF)
    acc_a[...] += mm(dm_ref[0].T, dkey)
    acc_b[...] += mm(x.T, dvc)
    part_ref[0] = dmix_ref[0] + mm_nt(dvc, wb_ref[...])
    fill_strips(ds_s, ddepth, length)
    fill_strips(xs_s, x, length)
    for strip in range(features // LANES):
        lanes = slice(strip * LANES, (strip + 1) * LANES)
        sums = [None] * KERNEL
        for at in range(0, length, piece):
            total = part_ref[0, at : at + piece, lanes]
            center = ds_s[strip, PAD + at : PAD + at + piece, :]
            for tap in range(KERNEL):
                begin = PAD + RADIUS - tap + at
                total = total + ds_s[strip, begin : begin + piece, :] * depth_ref[tap : tap + 1, lanes]
                begin = PAD - RADIUS + tap + at
                term = (xs_s[strip, begin : begin + piece, :] * center).reshape(-1, SLAB, LANES)
                term = jnp.sum(term, axis=0)
                sums[tap] = term if sums[tap] is None else sums[tap] + term
            part_ref[0, at : at + piece, lanes] = total
        for tap in range(KERNEL):
            small_ref[tap : tap + 1, lanes] += rowsum(sums[tap])

    @pl.when(step == pl.num_programs(0) - 1)
    def _():
        grad_ref[0] = acc_a[...].astype(BF)
        grad_ref[1] = acc_b[...].astype(BF)


def conv_back(place, hidden, dcat, dmix, kept, weights, rows):
    length, features = hidden.shape[1:]
    width = HEADS * HEAD_SIZE

    def by_row(array):
        zeros = (0,) * (array.ndim - 1)
        return pl.BlockSpec((1,) + array.shape[1:], lambda r, p: (r,) + zeros)

    outs = [
        (
            jax.ShapeDtypeStruct((rows, length, features), F32),
            pl.BlockSpec((1, length, features), lambda r, p: (r, 0, 0)),
        ),
        (
            jax.ShapeDtypeStruct((rows, length, width), BF),
            pl.BlockSpec((1, length, width), lambda r, p: (r, 0, 0)),
        ),
        (
            jax.ShapeDtypeStruct((2, features, width), BF),
            pl.BlockSpec((2, features, width), lambda r, p: (0, 0, 0)),
        ),
        (
            jax.ShapeDtypeStruct((16, features), F32),
            pl.BlockSpec((16, features), lambda r, p: (0, 0)),
        ),
        (
            jax.ShapeDtypeStruct((LANES, width + LANES), F32),
            pl.BlockSpec((LANES, width + LANES), lambda r, p: (0, 0)),
        ),
    ]
    strips = features // LANES
    return pl.pallas_call(
        conv_back_kernel,
        out_shape=[o[0] for o in outs],
        grid_spec=pltpu.PrefetchScalarGridSpec(
            num_scalar_prefetch=1,
            grid=(rows,),
            in_specs=[
                pl.BlockSpec((1, length, features), lambda r, p: (p[0] + r, 0, 0)),
                pl.BlockSpec((1, length, width), lambda r, p: (r, 0, 1)),
                by_row(dmix),
                *[by_row(a) for a in kept],
                *[whole(w) for w in weights],
            ],
            out_specs=[o[1] for o in outs],
            scratch_shapes=[
                pltpu.VMEM((width // LANES, length + 2 * PAD, LANES), F32),
                pltpu.VMEM((strips, length + 2 * PAD, LANES), F32),
                pltpu.VMEM((KERNEL * width // LANES, length + 2 * PAD, LANES), F32),
                pltpu.VMEM((strips, length + 2 * PAD, LANES), F32),
                pltpu.VMEM((length, KERNEL * width), BF),
                pltpu.VMEM((features, width), F32),
                pltpu.VMEM((features, width), F32),
            ],
        ),
        compiler_params=pltpu.CompilerParams(vmem_limit_bytes=VMEM_LIMIT),
        name="convolution_backward",
    )(place, hidden, dcat, dmix, *kept, *weights)


def att_back_kernel(
    place,
    x_ref,
    dcat_ref,
    datt_ref,
    part_ref,
    dqc_ref,
    q_ref,
    k_ref,
    v_ref,
    probs_ref,
    att_t_ref,
    wq_ref,
    wk_ref,
    wv_ref,
    own_ref,
    send_ref,
    grad_ref,
    small_ref,
    kt_s,
    dqt_s,
    dk_s,
    dv_s,
    total_s,
    acc_s,
):
    step = pl.program_id(0)
    length, features = x_ref.shape[1:]
    width = HEADS * HEAD_SIZE

    @pl.when(step == 0)
    def _():
        acc_s[...] = jnp.zeros_like(acc_s)
        small_ref[...] = jnp.zeros_like(small_ref)

    scaled_keys = (k_ref[0].astype(F32) * (HEAD_SIZE**-0.5)).astype(BF)
    kt_s[...] = scaled_keys.T
    low_lane = lax.broadcasted_iota(jnp.int32, (1, LANES), 1) < HEAD_SIZE
    for pair in range(HEADS // 2):
        lanes = slice(pair * LANES, (pair + 1) * LANES)
        d_pair = dcat_ref[0, :, lanes]
        q_pair = q_ref[0, :, lanes]
        v_pair = v_ref[0, :, lanes]
        dk = jnp.zeros((length, LANES), F32)
        dv = jnp.zeros((length, LANES), F32)
        for head in (2 * pair, 2 * pair + 1):
            span = slice(head * HEAD_SIZE, (head + 1) * HEAD_SIZE)
            keep = low_lane if head % 2 == 0 else jnp.logical_not(low_lane)
            d_own = datt_ref[0, span, :].astype(F32)
            delta = rowsum(d_own * att_t_ref[0, span, :].astype(F32))
            dp = mm(v_pair, head_pair_rows(datt_ref[0], head))
            probs = probs_ref[0, head]
            dscores = (probs.astype(F32) * (dp - delta)).astype(BF)
            dqt_s[span, :] = mm(kt_s[span, :], dscores)
            dv = dv + mm(probs, jnp.where(keep, d_pair, jnp.zeros_like(d_pair)))
            dk = dk + mm(dscores, jnp.where(keep, q_pair, jnp.zeros_like(q_pair)))
        dk_s[:, lanes] = dk.astype(BF)
        dv_s[:, lanes] = dv.astype(BF)
    dq = dqt_s[...].T.astype(BF).astype(F32) + dqc_ref[0].astype(F32)
    small_ref[0:1, 0:width] += rowsum(dq)
    small_ref[0:1, width : 2 * width] += rowsum(dv_s[...].astype(F32))
    dq = dq.astype(BF)
    x_t = x_ref[0].T
    acc_s[0] += mm(x_t, dq)
    acc_s[1] += mm(x_t, dk_s[...])
    acc_s[2] += mm(x_t, dv_s[...])
    total_s[...] = (
        part_ref[0]
        + mm_nt(dq, wq_ref[...])
        + mm_nt(dk_s[...], wk_ref[...])
        + mm_nt(dv_s[...], wv_ref[...])
    )
    half = length // 2
    mine = pl.multiple_of(place[1] * half, half)
    other = pl.multiple_of((1 - place[1]) * half, half)
    own_ref[0] = total_s[pl.ds(mine, half), :]
    send_ref[0] = total_s[pl.ds(other, half), :].astype(BF)

    @pl.when(step == pl.num_programs(0) - 1)
    def _():
        grad_ref[...] = acc_s[...].astype(BF)


def att_back(place, hidden, dcat, datt, part, dqc, kept, weights, rows):
    length, features = hidden.shape[1:]
    width = HEADS * HEAD_SIZE
    half = length // 2

    def by_row(array):
        zeros = (0,) * (array.ndim - 1)
        return pl.BlockSpec((1,) + array.shape[1:], lambda r, p: (r,) + zeros)

    outs = [
        (
            jax.ShapeDtypeStruct((rows, half, features), F32),
            pl.BlockSpec((1, half, features), lambda r, p: (r, 0, 0)),
        ),
        (
            jax.ShapeDtypeStruct((rows, half, features), BF),
            pl.BlockSpec((1, half, features), lambda r, p: (r, 0, 0)),
        ),
        (
            jax.ShapeDtypeStruct((3, features, width), BF),
            pl.BlockSpec((3, features, width), lambda r, p: (0, 0, 0)),
        ),
        (
            jax.ShapeDtypeStruct((SLAB, features), F32),
            pl.BlockSpec((SLAB, features), lambda r, p: (0, 0)),
        ),
    ]
    return pl.pallas_call(
        att_back_kernel,
        out_shape=[o[0] for o in outs],
        grid_spec=pltpu.PrefetchScalarGridSpec(
            num_scalar_prefetch=1,
            grid=(rows,),
            in_specs=[
                pl.BlockSpec((1, length, features), lambda r, p: (p[0] + r, 0, 0)),
                pl.BlockSpec((1, length, width), lambda r, p: (r, 0, 0)),
                by_row(datt),
                by_row(part),
                by_row(dqc),
                *[by_row(a) for a in kept],
                *[whole(w) for w in weights],
            ],
            out_specs=[o[1] for o in outs],
            scratch_shapes=[
                pltpu.VMEM((width, length), BF),
                pltpu.VMEM((width, length), F32),
                pltpu.VMEM((length, width), BF),
                pltpu.VMEM((length, width), BF),
                pltpu.VMEM((length, features), F32),
                pltpu.VMEM((3, features, width), F32),
            ],
        ),
        compiler_params=pltpu.CompilerParams(vmem_limit_bytes=VMEM_LIMIT),
        name="attention_backward",
    )(place, hidden, dcat, datt, part, dqc, *kept, *weights)


def shards(
    hidden,
    bounds,
    query_weight,
    query_bias,
    branch_keys,
    branch_values,
    branch_bias,
    depth_kernel,
    point_bias,
    kernel_weight,
    kernel_bias,
    mixer_weight,
    mixer_bias,
    first_gain,
    first_shift,
    inner_weight,
    inner_bias,
    outer_weight,
    outer_bias,
    second_gain,
    second_shift,
    cotangent,
):
    side = lax.axis_index("branch")
    both = ("branch", "dp")
    rows = hidden.shape[0] // 2
    half = cotangent.shape[1]
    features = hidden.shape[2]
    width = query_weight.shape[1]
    groups, _, inner = inner_weight.shape
    swap = [(0, 1), (1, 0)]

    def exchange(value):
        return lax.ppermute(value, "branch", swap)

    base = (side * rows).astype(jnp.int32)
    far = ((1 - side) * rows).astype(jnp.int32)
    own_weights = (branch_keys[0], branch_values[0], branch_bias)
    got_weights = tuple(exchange(w) for w in own_weights)
    cot_got = exchange(lax.dynamic_slice_in_dim(cotangent, far, rows, 0))

    def line(vector):
        return vector.reshape(1, -1)

    def by_tap(matrix):
        tapped = matrix.reshape(matrix.shape[0], HEADS, KERNEL).transpose(2, 1, 0)
        tapped = jnp.pad(tapped, ((0, 0), (0, SLAB - HEADS), (0, 0)))
        return tapped.reshape(KERNEL * SLAB, -1)

    kwt = jnp.pad(by_tap(kernel_weight), ((0, LANES - KERNEL * SLAB), (0, 0)))
    kb = jnp.pad(by_tap(kernel_bias[None, :]), ((0, LANES - KERNEL * SLAB), (0, LANES - 1)))
    spread = spread_table()
    common = (depth_kernel, line(point_bias), kwt, kb, spread)

    def run(order, weights, before):
        is_att = jnp.where(side == order, 1, 0).astype(jnp.int32)
        place = jnp.stack([base, is_att])
        return forward(
            place,
            bounds,
            hidden,
            (query_weight, line(query_bias), *weights, *common),
            rows,
            before,
        )

    kept = run(0, own_weights, None)
    kept = run(1, got_weights, kept)
    cat, q, k, v, probs, att_t, dm, kc, cq, joint, taps, vc = kept
    spot = jnp.stack([base, side.astype(jnp.int32)])
    out_own, out_send, dcat, datt, dmix, grad_mid, vec_mid = middle(
        spot,
        hidden,
        cat,
        cotangent,
        cot_got,
        (
            mixer_weight,
            line(mixer_bias),
            line(first_gain),
            line(first_shift),
            inner_weight,
            line(inner_bias),
            outer_weight,
            line(outer_bias),
            line(second_gain),
            line(second_shift),
        ),
        rows,
    )
    out_got = exchange(out_send)
    attend = tuple(jnp.where(side == 0, o, g) for o, g in zip(own_weights, got_weights))
    convolve = tuple(jnp.where(side == 0, g, o) for o, g in zip(own_weights, got_weights))
    part, dqc, grad_conv, small_conv, kgrad = conv_back(
        spot,
        hidden,
        dcat,
        dmix,
        (dm, kc, cq, joint, taps, vc),
        (convolve[0], convolve[1], depth_kernel, kwt, spread, gather_table()),
        rows,
    )
    hid_own, hid_send, grad_att, small_att = att_back(
        spot,
        hidden,
        dcat,
        datt,
        part,
        dqc,
        (q, k, v, probs, att_t),
        (query_weight, attend[0], attend[1]),
        rows,
    )
    hid_got = exchange(hid_send).astype(F32)

    def join(own, got):
        return jnp.where(
            side == 0, jnp.concatenate([own, got], 0), jnp.concatenate([got, own], 0)
        )

    output = join(out_own, out_got)
    hidden_grad = join(hid_own, hid_got)
    grad_mid = lax.psum(grad_mid, both).astype(F32)
    grad_conv, grad_att = lax.psum((grad_conv, grad_att), both)
    vec_mid, small_conv, kgrad, small_att = lax.psum(
        (vec_mid, small_conv, kgrad, small_att), both
    )
    rows_i = groups * width
    grad_inner = grad_mid[:rows_i].reshape(groups, width, inner)
    grad_outer = grad_mid[rows_i : 2 * rows_i].reshape(groups, width, inner).transpose(0, 2, 1)
    grad_mixer = jnp.concatenate(
        [grad_mid[2 * rows_i :, :features], grad_mid[2 * rows_i :, features:]], 0
    )
    keys = jnp.where(side == 0, grad_att[1], grad_conv[0]).astype(F32)[None]
    values = jnp.where(side == 0, grad_att[2], grad_conv[1]).astype(F32)[None]
    value_bias = jnp.where(side == 0, small_att[0, width : 2 * width], small_conv[9, width : 2 * width])[None]
    kernel_grads = kgrad[: KERNEL * SLAB].reshape(KERNEL, SLAB, -1)[:, :HEADS].transpose(1, 0, 2)
    kernel_grads = kernel_grads.reshape(HEADS * KERNEL, -1)
    return (
        output,
        hidden_grad,
        grad_att[0].astype(F32),
        small_att[0, :width],
        keys,
        values,
        value_bias,
        small_conv[:KERNEL],
        small_conv[9, :width],
        kernel_grads[:, :width].T,
        kernel_grads[:, width],
        grad_mixer,
        vec_mid[1, :features],
        vec_mid[1, features : 2 * features],
        vec_mid[1, 2 * features : 3 * features],
        grad_inner,
        vec_mid[0],
        grad_outer,
        vec_mid[1, 3 * features : 4 * features],
        vec_mid[2, :features],
        vec_mid[2, features : 2 * features],
    )


def solution(mesh):
    split = P("dp", "branch", None)
    owned = P("branch", None, None)
    return jax.shard_map(
        shards,
        mesh=mesh,
        in_specs=(
            P("dp", None, None),
            P("dp", None),
            P(),
            P(),
            owned,
            owned,
            P("branch", None),
            *([P()] * 14),
            split,
        ),
        out_specs=(
            split,
            split,
            P(),
            P(),
            owned,
            owned,
            P("branch", None),
            *([P()] * 14),
        ),
        check_vma=False,
    )
```

time: 731 us -> 637 us (0.87)
  matrix products: 206 us -> 0 us
  waiting for transfers between devices: 271 us -> 435 us
  Pallas kernels: 0 us -> 126 us
  blocking collectives: 116 us -> 0 us
  local copies, waits for them, and re-layouts: 62.3 us -> 32.5 us
  other arithmetic: 41.1 us -> 14 us
    psum x2 -> x3, waiting for transfers between devices: 250 us -> 434 us  [the longest x2 249 us: shards(): lax.psum((vec_mid, small_conv, kgrad, small_att), both)]
    dot_general x26 -> x0, matrix products: 175 us -> none  [the longest x2 36.4 us: grouped(): jnp.einsum('rsgi,gio->rsgo', split_source, matrix, preferred_element_type...]
    pallas_call x0 -> x5, Pallas kernels: none -> 126 us  [the longest x1 50.2 us: middle(): pl.pallas_call(middle_kernel, out_shape=[o[0] for o in outs], grid_spec=p...]
    psum x2 -> x0, blocking collectives: 94.1 us -> none  [the longest x1 62.5 us: shards(): lax.psum((grad_query_weight, grad_query_bias, grad_mixer_weight, grad_mix...]
    sub x2 -> x0, matrix products: 31 us -> none  [softmax_last(): raised = jnp.exp(scores - row_peak)]
    all_to_all x1 -> x0, blocking collectives: 21.7 us -> none  [shards(): lax.all_to_all(grad_concat, 'branch', split_axis=2, concat_axis=1, tiled=...]
    convert_element_type x2, other arithmetic: 23.1 us -> 2.01 us  [the longest x1 1.91 us: shards(): values = jnp.where(side == 0, grad_att[2], grad_conv[1]).astype(F32)[None]]
    all_to_all x1 -> x0, waiting for transfers between devices: 20.8 us -> none  [shards(): lax.all_to_all(branch_out, 'branch', split_axis=1, concat_axis=2, tiled=T...]
  transfers between devices with their start and end apart: 4 -> 9, of which waited for: 3 -> 3; matrix products, arithmetic and copies ran while one was open for 4% -> 4% of each run, Pallas kernels for 0% -> 5%
where the time goes in v1:
time: 637 us; the launch traced here: 630 us
  waiting for transfers between devices  435 us (68%)
  Pallas kernels  126 us (20%)
  local copies, waits for them, and re-layouts  32.5 us (5%)
  between operations  14.3 us (2%)
  other arithmetic  14 us (2%)
  starting transfers between devices  7.67 us (1%)
    psum x2, waiting for transfers between devices, shards(): lax.psum((vec_mid, small_conv, kgrad, small_att), both)  249 us
    psum x1, waiting for transfers between devices, shards(): grad_conv, grad_att = lax.psum((grad_conv, grad_att), both)  184 us
    pallas_call x1, Pallas kernels, middle(): pl.pallas_call(middle_kernel, out_shape=[o[0] for o in outs], grid_spec=p...  50.2 us
    pallas_call x2, Pallas kernels, forward(): pl.pallas_call(forward_kernel, out_shape=[o[0] for o in outs], grid_spec=...  33.1 us
    pallas_call x1, Pallas kernels, conv_back(): pl.pallas_call(conv_back_kernel, out_shape=[o[0] for o in outs], grid_spe...  23 us
    pallas_call x1, Pallas kernels, att_back(): pl.pallas_call(att_back_kernel, out_shape=[o[0] for o in outs], grid_spec...  20.1 us
  transfers between devices with their start and end apart: 9, of which 3 were waited for; matrix products, arithmetic and copies ran while one was open for 4% of the time, Pallas kernels for 5%

profile of v1, /device:TPU:0, one launch (start us, length us, event | category | flops | bytes accessed | tf_op | source)
XLA Modules:
  0.0 629.8 jit_solution(13845493696980701180)
XLA Ops:
  7.4 3.0 collective-permute-start
  10.5 1.9 collective-permute-start.2
  12.4 2.1 constant_dynamic-slice_fusion
  23.2 16.8 %branch_forward.2 = (bf16[2,512,768]{2,1,0:T(8,128)(2,1)}, bf16[3,512,384]{2,1,0:T(8,128)(2,1)}, bf16[3,512,384]{2,1,0:T(8,128)(2,1)}, bf16[3,512,384]{2,1,0:T(8...) custom-call(s32[2]{0:T(128)} %pad_add_fusion.2.place, ...), custom_call_target="tpu_custom_call" | custom-call | tf_op jit(solution)/shard_map/branch_forward/pallas_call | solution.py:261
  41.1 16.3 %branch_forward.3 = (bf16[2,512,768]{2,1,0:T(8,128)(2,1)}, bf16[3,512,384]{2,1,0:T(8,128)(2,1)}, bf16[3,512,384]{2,1,0:T(8,128)(2,1)}, bf16[3,512,384]{2,1,0:T(8...) custom-call(s32[2]{0:T(128)} %pad_add_fusion.1.place, ...), custom_call_target="tpu_custom_call", output_to_operand_aliasing={{0}: (13, {}), {1}: (14, {}), {2}: (15, {}), {3}: (16, {}),... | custom-call | tf_op jit(solution)/shard_map/branch_forward/pallas_call | solution.py:261
  57.4 2.3 broadcast_select_fusion
  59.7 1.1 broadcast_select_fusion.1
  60.8 50.2 %shared_layers.1 = (bf16[2,256,768]{2,1,0:T(8,128)(2,1)}, bf16[2,256,768]{2,1,0:T(8,128)(2,1)}, bf16[2,512,768]{2,1,0:T(8,128)(2,1)}, bf16[2,384,512]{2,1,0:T(8,...) custom-call(s32[2]{0:T(128)} %pad_add_fusion.place, bf16[4,512,768]{2,1,0:T(8,128)(2,1)} %x_ref.9, ...), custom_call_target="tpu_custom_call" | custom-call | tf_op jit(solution)/shard_map/shared_layers/pallas_call | solution.py:446
  111.0 23.0 %convolution_backward.1 = (f32[2,512,768]{2,1,0:T(8,128)}, bf16[2,512,384]{2,1,0:T(8,128)(2,1)}, bf16[2,768,384]{2,1,0:T(8,128)(2,1)}, f32[16,768]{1,0:T(8,128)}, f32[128,512]{1,0:T(8,128)}) custom-call(s32[2]{0:T(128)} %pad_add_fusion.place, bf16[4,512,768]{2,1,0:T(8,128)(2,1)} %x_ref.9, bf16[2,512,768]{2,1,0:T(8,128)(2,1)} %get-tuple-element.76.dcat_ref, ...), custom_call_target="tpu_custom_call" | custom-call | tf_op jit(solution)/shard_map/convolution_backward/pallas_call | solution.py:624
  134.1 20.1 %attention_backward.1 = (f32[2,256,768]{2,1,0:T(8,128)}, bf16[2,256,768]{2,1,0:T(8,128)(2,1)}, bf16[3,768,384]{2,1,0:T(8,128)(2,1)}, f32[8,768]{1,0:T(8,128)}) custom-call(s32[2]{0:T(128)} %pad_add_fusion.place, bf16[4,512,768]{2,1,0:T(8,128)(2,1)} %x_ref.9, bf16[2,512,768]{2,1,0:T(8,128)(2,1)} %get-tuple-element.76.dcat_ref, ...), custom_call_target="tpu_custom_call" | custom-call | tf_op jit(solution)/shard_map/attention_backward/pallas_call | solution.py:763
  155.7 2.0 collective-permute-start.5
  158.1 116.7 %all-reduce.11.cloned.1.call-done = (f32[8,768]{1,0:T(8,128)}, f32[16,768]{1,0:T(8,128)}) async-done(((f32[8,768]{1,0:T(8,128)}, f32[16,768]{1,0:T(8,128)}), (f32[8,768]{1,0:T(8,128)}, f32[16,768]{1,0:T(8,128)})) %all-reduce.11.cloned.1.call-update) | async-done | bytes 73744 | tf_op jit(solution)/shard_map/psum | solution.py:918
  274.8 1.9 slice_reduce_fusion.7
  276.7 132.5 %all-reduce.13.cloned.1.call-done = (f32[128,512]{1,0:T(8,128)}, f32[8,3072]{1,0:T(8,128)}) async-done(((f32[128,512]{1,0:T(8,128)}, f32[8,3072]{1,0:T(8,128)}), (f32[128,512]{1,0:T(8,128)}, f32[8,3072]{1,0:T(8,128)})) %all-reduce.13.cloned.1.call-update) | async-done | bytes 360464 | tf_op jit(solution)/shard_map/psum | solution.py:918
  410.2 1.6 slice.120
  412.4 1.5 slice_reduce_fusion.1
  414.7 1.4 maximum_select_fusion.1
  416.6 2.0 maximum_select_fusion
  418.6 184.3 %all-reduce.15.cloned.1.call-done = (bf16[3,768,384]{2,1,0:T(8,128)(2,1)}, bf16[2,768,384]{2,1,0:T(8,128)(2,1)}, bf16[1920,1536]{1,0:T(8,128)(2,1)}) async-done(((bf16[3,768,384]{2,1,0:T(8,128)(2,1)}, bf16[2,768,384]{2,1,0:T(8,128)(2,1)}, bf16[1920,1536]{1,0:T(8,128)(2,1)}), (bf16[3,768,384]{2,1,0:T(8,128)(2,1)}, bf16[2,768,384]{2,1,0:T(8,128)(2,1)}, ...) | async-done | bytes 8847376 | tf_op jit(solution)/shard_map/psum | solution.py:917
  602.9 7.4 %fusion.3 = (f32[768,1536]{1,0:T(8,128)}, f32[768,1536]{1,0:T(8,128)}) fusion(bf16[1920,1536]{1,0:T(8,128)(2,1)} %get-tuple-element.113), kind=kLoop, calls=%fused_computation.31 | loop fusion | bytes 18874368 | tf_op jit(solution)/shard_map/slice | solution.py:923
  610.4 1.4 fusion.4
  611.8 6.0 copy.70
  617.9 1.6 pad_maximum_fusion
  620.5 1.9 fusion
  (89 shorter events, 16.4 us)
Async XLA Ops:
  7.2 7.4 %copy-start.10 = (bf16[384,54]{0,1:T(8,128)(2,1)S(1)}, bf16[384,54]{0,1:T(8,128)(2,1)}, u32[]{:S(2)}) copy-start(bf16[384,54]{0,1:T(8,128)(2,1)} %param.33) | copy-start | bytes 124420
  7.2 7.4 %copy-start.21 = (f32[54]{0:T(128)S(1)}, f32[54]{0:T(128)}, u32[]{:S(2)}) copy-start(f32[54]{0:T(128)} %param.34) | copy-start | bytes 652
  7.2 10.1 %copy-start.20 = (s32[4,2]{0,1:T(2,128)S(1)}, s32[4,2]{0,1:T(2,128)}, u32[]{:S(2)}) copy-start(s32[4,2]{0,1:T(2,128)} %param.25) | copy-start | bytes 100
  7.2 10.7 %copy-start.17 = (f32[384]{0:T(512)S(1)}, f32[384]{0:T(512)}, u32[]{:S(2)}) copy-start(f32[384]{0:T(512)} %param.27) | copy-start | bytes 4612
  7.2 11.3 %copy-start.18 = (f32[384]{0:T(512)S(1)}, f32[384]{0:T(512)}, u32[]{:S(2)}) copy-start(f32[384]{0:T(512)} %param.32) | copy-start | bytes 4612
  7.2 11.8 %copy-start.11 = (f32[768]{0:T(1024)S(1)}, f32[768]{0:T(1024)}, u32[]{:S(2)}) copy-start(f32[768]{0:T(1024)} %param.38) | copy-start | bytes 9220
  7.3 12.4 %copy-start.12 = (f32[768]{0:T(1024)S(1)}, f32[768]{0:T(1024)}, u32[]{:S(2)}) copy-start(f32[768]{0:T(1024)} %param.42) | copy-start | bytes 9220
  7.3 13.0 %copy-start.13 = (f32[768]{0:T(1024)S(1)}, f32[768]{0:T(1024)}, u32[]{:S(2)}) copy-start(f32[768]{0:T(1024)} %param.43) | copy-start | bytes 9220
  7.3 13.6 %copy-start.14 = (f32[768]{0:T(1024)S(1)}, f32[768]{0:T(1024)}, u32[]{:S(2)}) copy-start(f32[768]{0:T(1024)} %param.44) | copy-start | bytes 9220
  7.3 14.1 %copy-start.15 = (f32[768]{0:T(1024)S(1)}, f32[768]{0:T(1024)}, u32[]{:S(2)}) copy-start(f32[768]{0:T(1024)} %param.36) | copy-start | bytes 9220
  7.3 14.7 %copy-start.16 = (f32[768]{0:T(1024)S(1)}, f32[768]{0:T(1024)}, u32[]{:S(2)}) copy-start(f32[768]{0:T(1024)} %param.37) | copy-start | bytes 9220
  7.3 267.5 %all-reduce.11.cloned.1.call-start = ((), (), s32[]{:S(2)}) async-start(), calls=%async_computation | async-start | bytes 147456 | tf_op jit(solution)/shard_map/psum | solution.py:918
  7.4 32.7 %collective-permute-start = (bf16[768,384]{1,0:T(8,128)(2,1)}, bf16[768,384]{1,0:T(8,128)(2,1)S(1)}, u32[]{:S(2)}, u32[]{:S(2)}) collective-permute-start(bf16[768,384]{1,0:T(8,128)(2,1)} %bitcast.42), channel_id=1, source_target_pairs={{0,16},{16,0},{1,17},{17,1},{2,18},{18,2},{3,19},{19,3},{4,20},{20... | collective-permute-start | bytes 1769480 | tf_op jit(solution)/shard_map/ppermute | solution.py:827
  10.4 29.7 %collective-permute-start.1 = (bf16[768,384]{1,0:T(8,128)(2,1)}, bf16[768,384]{1,0:T(8,128)(2,1)S(1)}, u32[]{:S(2)}, u32[]{:S(2)}) collective-permute-start(bf16[768,384]{1,0:T(8,128)(2,1)} %bitcast.40), channel_id=1, source_target_pairs={{0,16},{16,0},{1,17},{17,1},{2,18},{18,2},{3,19},{19,3},{4,20},{20... | collective-permute-start | bytes 1769480 | tf_op jit(solution)/shard_map/ppermute | solution.py:827
  10.5 29.6 %collective-permute-start.2 = (f32[1,384]{1,0:T(1,128)}, f32[1,384]{1,0:T(1,128)S(1)}, u32[]{:S(2)}, u32[]{:S(2)}) collective-permute-start(f32[1,384]{1,0:T(1,128)} %bb_ref.1), channel_id=1, source_target_pairs={{0,16},{16,0},{1,17},{17,1},{2,18},{18,2},{3,19},{19,3},{4,20},{20... | collective-permute-start | bytes 4616 | tf_op jit(solution)/shard_map/ppermute | solution.py:827
  14.5 46.4 %collective-permute-start.3 = (bf16[2,256,768]{2,1,0:T(8,128)(2,1)}, bf16[2,256,768]{2,1,0:T(8,128)(2,1)}, u32[]{:S(2)}, u32[]{:S(2)}) collective-permute-start(bf16[2,256,768]{2,1,0:T(8,128)(2,1)} %constant_dynamic-slice_fusion), channel_id=1, source_target_pairs={{0,16},{16,0},{1,17},{17,1},{2,18},{18,2},{3,19},{19,3},{4,20},{20... | collective-permute-start | bytes 2359304 | tf_op jit(solution)/shard_map/ppermute | solution.py:827
  41.1 16.3 %copy-start = (bf16[1,768,384]{2,1,0:T(8,128)(2,1)S(1)}, bf16[1,768,384]{2,1,0:T(8,128)(2,1)}, u32[]{:S(2)}) copy-start(bf16[1,768,384]{2,1,0:T(8,128)(2,1)} %param.29) | copy-start | bytes 1769476
  154.2 255.0 %all-reduce.13.cloned.1.call-start = ((), (), s32[]{:S(2)}) async-start(), calls=%async_computation.1 | async-start | bytes 720896 | tf_op jit(solution)/shard_map/psum | solution.py:918
  155.0 448.0 %all-reduce.15.cloned.1.call-start = ((), (), s32[]{:S(2)}) async-start(), calls=%async_computation.2 | async-start | bytes 17694720 | tf_op jit(solution)/shard_map/psum | solution.py:917
  155.0 2.7 copy-start.22
  155.7 258.9 %collective-permute-start.5 = (bf16[2,256,768]{2,1,0:T(8,128)(2,1)}, bf16[2,256,768]{2,1,0:T(8,128)(2,1)S(1)}, u32[]{:S(2)}, u32[]{:S(2)}) collective-permute-start(bf16[2,256,768]{2,1,0:T(8,128)(2,1)} %get-tuple-element.93), channel_id=1, source_target_pairs={{0,16},{16,0},{1,17},{17,1},{2,18},{18,2},{3,19},{19,3},{4,20},{20... | collective-permute-start | bytes 2359304 | tf_op jit(solution)/shard_map/ppermute | solution.py:827
  157.7 257.0 %collective-permute-start.4 = (bf16[2,256,768]{2,1,0:T(8,128)(2,1)S(1)}, bf16[2,256,768]{2,1,0:T(8,128)(2,1)S(1)}, u32[]{:S(2)}, u32[]{:S(2)}) collective-permute-start(bf16[2,256,768]{2,1,0:T(8,128)(2,1)S(1)} %copy-done.22), channel_id=1, source_target_pairs={{0,16},{16,0},{1,17},{17,1},{2,18},{18,2},{3,19},{19,3},{4,20},{20... | collective-permute-start | bytes 2359304 | tf_op jit(solution)/shard_map/ppermute | solution.py:827
  410.1 4.6 copy-start.8
  617.9 2.7 copy-start.7
  (8 other events, 13.2 us)
Sparse Core Ops, SparseCore 0:
  154.3 120.4 all-reduce.10
  280.2 128.9 all-reduce.12
  417.1 185.7 all-reduce.14
